TPU v7x, 32 devices: a whole 2x2x4 slice. The times are simulated.
32 devices in a mesh: region: 8 (over z, core), group: 4 (over y, x).
Axes of the slice: x: 2, y: 2, z: 4, core: 2. Of those that a mesh axis runs over, the one named last changes fastest.
Arguments:
- features: bfloat16 [12288, 2048], P(('region', 'group')), may hold values from -1.5 to 1.5
- memory: bfloat16 [4096, 2048], P(('region', 'group')), may hold values from -1 to 1
- requests: int32 [32, 2], P(('region', 'group')), may hold values from 0 to 3, as said below
- owners: int32 [8, 4], P('region'), may hold values from 0 to 3, as said below
- labels: int32 [32, 384], P(('region', 'group')), may hold values from 0 to 1023, as said below
Outputs:
- feat_grad: bfloat16 [12288, 2048], P(('region', 'group'))
- new_memory: bfloat16 [4096, 2048], P(('region', 'group'))
Inputs may be any that keep to these rules, and one draw needn't show every extreme that they name: `owners`: each row of a region is a permutation. `requests`: the 2 numbers of a device are distinct blocks of its region. At most 96 crops of one device carry labels of one region, and every device reaches that bound for some region.
All inputs are finite; a program needn't handle non-finite values.
Results may differ from a plain program's by a relative error of at most 0.006.
Values may be sent and summed in bfloat16 or wider, within the bound.
No kernel may reach another device: no remote copies, remote signals or barrier semaphores. Data moves between devices by JAX's collectives and lax.ppermute only.
A program may use at most 64 MiB of HBM per device.

v0:
```python
import jax
import jax.numpy as jnp
from jax import lax
from jax.sharding import PartitionSpec as P

D = 2048


exponent_sharpness = 0.05
smoothing = 0.1
momentum_keep = 0.2


def on_device(features, memory, requests, owners, labels):
    group_count = lax.axis_size("group")
    region_count = lax.axis_size("region")
    block_rows = memory.shape[0]
    feat_width = memory.shape[1]
    crop_count = features.shape[0]
    wanted_owner = jnp.take(owners[0], requests[0], axis=0)
    arrived = lax.all_gather(memory, "group", axis=0, tiled=True).reshape(
        group_count, block_rows, feat_width
    )
    reciprocal_memory_slices = jnp.take(arrived, wanted_owner, axis=0).reshape(-1, feat_width)
    cand_count = reciprocal_memory_slices.shape[0]
    cosine_affinities = (
        lax.dot_general(
            features,
            reciprocal_memory_slices,
            (((1,), (1,)), ((), ())),
            preferred_element_type=jnp.float32,
        )
        / exponent_sharpness
    )
    shifted = cosine_affinities - jnp.max(cosine_affinities, axis=1, keepdims=True)
    expo = jnp.exp(shifted)
    normalized_likelihoods = expo / jnp.sum(expo, axis=1, keepdims=True)
    column = jnp.arange(cand_count, dtype=jnp.int32)
    smoothed_identity_weights = (
        jnp.where(column < block_rows, (1.0 - smoothing) / block_rows, 0.0) + smoothing / cand_count
    ).astype(jnp.float32)
    pre_normalized_derivative = (
        (normalized_likelihoods - smoothed_identity_weights[None, :]) / exponent_sharpness
    ).astype(jnp.bfloat16)
    feat_grad = jnp.dot(
        pre_normalized_derivative, reciprocal_memory_slices, preferred_element_type=jnp.float32
    ).astype(jnp.bfloat16)
    capacity = max(2, 2 * crop_count // region_count)
    label_row = labels[0]
    label_region = label_row // block_rows
    label_offset = label_row % block_rows
    region_onehot = (
        label_region[:, None] == jnp.arange(region_count, dtype=jnp.int32)[None, :]
    ).astype(jnp.int32)
    earlier = jnp.sum((jnp.cumsum(region_onehot, axis=0) - region_onehot) * region_onehot, axis=1)
    slot_of = label_region * capacity + earlier
    slot_match = jnp.arange(region_count * capacity, dtype=jnp.int32)[:, None] == slot_of[None, :]
    packed = jnp.dot(
        slot_match.astype(jnp.bfloat16), features, preferred_element_type=jnp.float32
    ).astype(jnp.bfloat16)
    packed = packed.reshape(region_count, capacity, feat_width)
    slot_offsets = (
        jnp.sum(jnp.where(slot_match, label_offset[None, :] + 1, 0), axis=1) - 1
    ).reshape(region_count, capacity)
    received, received_offsets = (
        lax.all_to_all(packed, "region", split_axis=0, concat_axis=0, tiled=True),
        lax.all_to_all(slot_offsets, "region", split_axis=0, concat_axis=0, tiled=True),
    )
    received_rows = received.reshape(-1, feat_width)
    row_match = (
        jnp.arange(block_rows, dtype=jnp.int32)[:, None] == received_offsets.reshape(-1)[None, :]
    )
    sums = jnp.dot(
        row_match.astype(jnp.bfloat16), received_rows, preferred_element_type=jnp.float32
    )
    counts = jnp.sum(row_match.astype(jnp.float32), axis=1)
    old_rows = memory.astype(jnp.float32)
    averaged = sums / jnp.maximum(counts, 1.0)[:, None]
    mixed = jnp.where(
        counts[:, None] > 0, momentum_keep * old_rows + (1.0 - momentum_keep) * averaged, old_rows
    )
    scale = lax.rsqrt(jnp.mean(mixed * mixed, axis=1, keepdims=True) + 1e-06) * D ** (-0.5)
    new_memory = (mixed * scale).astype(jnp.bfloat16)
    return (feat_grad, new_memory)


def solution(mesh):
    placed = (
        P(("region", "group"), None),
        P(("region", "group"), None),
        P(("region", "group"), None),
        P("region", None),
        P(("region", "group"), None),
    )
    return jax.shard_map(
        on_device,
        mesh=mesh,
        in_specs=placed,
        out_specs=(P(("region", "group"), None), P(("region", "group"), None)),
        check_vma=False,
    )
```

profile of v0, /device:TPU:0, one launch (start us, length us, event | category | flops | bytes accessed | tf_op | source)
XLA Modules:
  0.0 109.4 jit_solution(12788374351768573846)
XLA Ops:
  7.2 0.0 copy-start
  7.2 0.8 reduce.2
  8.0 0.9 reduce-window.6
  8.9 0.2 slice_reduce_fusion
  9.2 0.1 fusion.11
  9.3 0.7 fusion.19
  10.0 0.2 select_reduce_fusion
  10.2 0.7 sub.45
  10.9 6.3 %all-to-all-start = ((s32[8,1,96]{2,1,0:T(1,128)}), s32[8,1,96]{2,1,0:T(1,128)S(1)}, u32[]{:S(2)}, u32[]{:S(2)}) async-start(s32[8,1,96]{2,1,0:T(1,128)} %sub.45), calls=%async_computation | async-start | bytes 8192 | tf_op jit(solution)/shard_map/all_to_all | solution.py:67
  17.2 0.0 copy-done
  17.2 3.5 %convolution_convert_fusion = bf16[768,2048]{1,0:T(8,128)(2,1)} fusion(bf16[384,2048]{1,0:T(8,128)(2,1)S(1)} %copy-done, s32[384]{0:T(512)S(1)} %get-tuple-element.3), kind=kOutput, calls=%fused_computation.2 | convolution fusion | flops 1209827328 | bytes 4720128 | tf_op jit(solution)/shard_map/dot_general | solution.py:58
  20.7 2.0 %all-to-all-done = s32[8,1,96]{2,1,0:T(1,128)S(1)} async-done(((s32[8,1,96]{2,1,0:T(1,128)}), s32[8,1,96]{2,1,0:T(1,128)S(1)}, u32[]{:S(2)}, u32[]{:S(2)}) %all-to-all-start) | async-done | bytes 3104 | tf_op jit(solution)/shard_map/all_to_all | solution.py:67
  22.7 0.0 copy-start.3
  22.7 0.0 copy-start.1
  22.7 4.6 %all-to-all-start.1 = ((bf16[8,96,2048]{2,1,0:T(8,128)(2,1)}), bf16[8,96,2048]{2,1,0:T(8,128)(2,1)}, u32[]{:S(2)}, u32[]{:S(2)}) async-start(bf16[8,96,2048]{2,1,0:T(8,128)(2,1)} %bitcast.57), calls=%async_computation.1 | async-start | bytes 6291456 | tf_op jit(solution)/shard_map/all_to_all | solution.py:66
  27.2 0.0 all-gather.2.cloned.1.call-start
  27.3 0.7 all-gather.2.cloned.1.call-update
  28.0 0.0 copy-done.3
  28.0 0.0 copy-done.1
  28.0 0.6 gather_fusion
  28.7 0.1 broadcast_bitcast_fusion
  28.8 0.5 broadcast.314
  29.3 0.7 reduce.13
  30.0 0.1 eq.64
  30.0 0.1 convert_reduce_fusion
  30.2 36.5 %all-gather.2.cloned.1.call-done = bf16[512,2048]{1,0:T(8,128)(2,1)} async-done(((bf16[128,2048]{1,0:T(8,128)(2,1)}), bf16[512,2048]{1,0:T(8,128)(2,1)}) %all-gather.2.cloned.1.call-update) | async-done | bytes 2097168 | tf_op jit(solution)/shard_map/all_gather | solution.py:21
  66.6 2.2 %gather_fusion.1 = bf16[2,128,2048]{2,1,0:T(8,128)(2,1)S(1)} fusion(bf16[4,128,2048]{2,1,0:T(8,128)(2,1)} %bitcast.58, s32[1024]{0:T(1024)S(1)} %pad_clamp_fusion), kind=kCustom, calls=%fused_computation.1 | custom fusion | bytes 2097160 | tf_op jit(solution)/shard_map/jit(_take)/gather | solution.py:24
  68.8 0.2 bitcast_select_fusion
  69.0 0.7 fusion.24
  69.8 0.1 fusion.4
  69.9 0.0 copy-start.2
  69.9 1.8 %convolution_convert_fusion.1 = bf16[384,2048]{1,0:T(8,128)(2,1)} fusion(bf16[256,2048]{1,0:T(8,128)(2,1)S(1)} %bitcast_select_fusion, f32[256,384]{1,0:T(8,128)S(1)} %get-tuple-element.5, f32[256]{0:T(256)S(1)} %fusion.20, f32[384]{0:T(512)S(1)} %fusion.4, f32[384]{0:T(512)S(1)} %get-tuple-element.4), kind=kOutput, calls=%fused_computation.3 | convolution fusion | flops 403931136 | bytes 3018752 | tf_op jit(solution)/shard_map/dot_general | solution.py:45
  71.7 27.0 %all-to-all-done.1 = bf16[8,96,2048]{2,1,0:T(8,128)(2,1)} async-done(((bf16[8,96,2048]{2,1,0:T(8,128)(2,1)}), bf16[8,96,2048]{2,1,0:T(8,128)(2,1)}, u32[]{:S(2)}, u32[]{:S(2)}) %all-to-all-start.1) | async-done | bytes 3145760 | tf_op jit(solution)/shard_map/all_to_all | solution.py:66
  98.8 0.0 copy-done.2
  98.8 2.8 %multiply_reduce_fusion = (f32[128]{0:T(128)S(1)}, f32[128,2048]{1,0:T(8,128)S(1)}) fusion(f32[128]{0:T(128)S(1)} %broadcast_maximum_fusion, bf16[768,2048]{1,0:T(8,128)(2,1)} %bitcast.12, s32[768]{0:T(1024)S(1)} %eq.64, bf16[128,2048]{1,0:T(8,128)(2,1)S(1)} %copy-done.2, pred[128]{0:T(512)(128)(4,1)S(1)} %broadcast_compare_fusion), kind=kOutput, calls=%fused_computation.14 | convolution fusion | flops 404848512 | bytes 4722816 | tf_op jit(solution)/shard_map/dot_general | solution.py:73
  101.6 0.9 multiply_convert_fusion
  (14 shorter events, 0.1 us)
Async XLA Ops:
  7.2 10.0 %copy-start = (bf16[384,2048]{1,0:T(8,128)(2,1)S(1)}, bf16[384,2048]{1,0:T(8,128)(2,1)}, u32[]{:S(2)}) copy-start(bf16[384,2048]{1,0:T(8,128)(2,1)} %param.5) | copy-start | bytes 4718596
  10.9 11.8 %all-to-all-start = ((s32[8,1,96]{2,1,0:T(1,128)}), s32[8,1,96]{2,1,0:T(1,128)S(1)}, u32[]{:S(2)}, u32[]{:S(2)}) async-start(s32[8,1,96]{2,1,0:T(1,128)} %sub.45), calls=%async_computation | async-start | bytes 8192 | tf_op jit(solution)/shard_map/all_to_all | solution.py:67
  22.7 5.3 %copy-start.3 = (s32[1,2]{1,0:T(1,128)S(1)}, s32[1,2]{1,0:T(1,128)}, u32[]{:S(2)}) copy-start(s32[1,2]{1,0:T(1,128)} %param.7) | copy-start | bytes 28
  22.7 5.4 %copy-start.1 = (s32[1,4]{1,0:T(1,128)S(1)}, s32[1,4]{1,0:T(1,128)}, u32[]{:S(2)}) copy-start(s32[1,4]{1,0:T(1,128)} %param.8) | copy-start | bytes 52
  22.7 76.1 %all-to-all-start.1 = ((bf16[8,96,2048]{2,1,0:T(8,128)(2,1)}), bf16[8,96,2048]{2,1,0:T(8,128)(2,1)}, u32[]{:S(2)}, u32[]{:S(2)}) async-start(bf16[8,96,2048]{2,1,0:T(8,128)(2,1)} %bitcast.57), calls=%async_computation.1 | async-start | bytes 6291456 | tf_op jit(solution)/shard_map/all_to_all | solution.py:66
  27.2 39.4 %all-gather.2.cloned.1.call-start = ((), (), s32[]{:S(2)}) async-start(), calls=%async_computation.2 | async-start | bytes 2621440 | tf_op jit(solution)/shard_map/all_gather | solution.py:21
  69.9 28.9 %copy-start.2 = (bf16[128,2048]{1,0:T(8,128)(2,1)S(1)}, bf16[128,2048]{1,0:T(8,128)(2,1)}, u32[]{:S(2)}) copy-start(bf16[128,2048]{1,0:T(8,128)(2,1)} %param.6) | copy-start | bytes 1572868
Sparse Core Ops, SparseCore 0:
  29.9 36.6 all-gather.1
where the time goes:
time: 110 us; the launch traced here: 109 us
  waiting for transfers between devices  66.2 us (60%)
  between operations  14.2 us (13%)
  starting transfers between devices  10.9 us (10%)
  matrix products  8.89 us (8%)
  other arithmetic  4.84 us (4%)
  local copies, waits for them, and re-layouts  4.41 us (4%)
    all_gather x1, waiting for transfers between devices, on_device(): lax.all_gather(memory, 'group', axis=0, tiled=True)  36.5 us
    all_to_all x1, waiting for transfers between devices, on_device(): lax.all_to_all(packed, 'region', split_axis=0, concat_axis=0, tiled=True)  27 us
    all_to_all x1, starting transfers between devices, on_device(): lax.all_to_all(slot_offsets, 'region', split_axis=0, concat_axis=0, tiled...  6.33 us
    all_to_all x1, starting transfers between devices, on_device(): lax.all_to_all(packed, 'region', split_axis=0, concat_axis=0, tiled=True)  4.57 us
    dot_general x1, matrix products, on_device(): jnp.dot(slot_match.astype(jnp.bfloat16), features, preferred_element_type...  3.5 us
    dot_general x1, matrix products, on_device(): jnp.dot(row_match.astype(jnp.bfloat16), received_rows, preferred_element_...  2.81 us
    gather x1, local copies, waits for them, and re-layouts, on_device(): jnp.take(arrived, wanted_owner, axis=0).reshape(-1, feat_width)  2.2 us
  transfers between devices with their start and end apart: 3, of which 3 were waited for; matrix products, arithmetic and copies ran while one was open for 10% of the time, Pallas kernels for 0%

commit v1 on v0

v1 whole, which is shorter than its diff:
```python
import jax
import jax.numpy as jnp
from jax import lax
from jax.sharding import PartitionSpec as P

D = 2048
CORES = 2

exponent_sharpness = 0.05
smoothing = 0.1
momentum_keep = 0.2


def on_device(features, memory, requests, owners, labels):
    group_count = lax.axis_size("group")
    region_count = lax.axis_size("region")
    layers = region_count // CORES
    block_rows, feat_width = memory.shape
    region = lax.axis_index("region")
    group = lax.axis_index("group")
    layer, core = region // CORES, region % CORES
    label_row = labels[0]

    def local_sums(which_core):
        row = jnp.arange(layers * block_rows, dtype=jnp.int32)
        value = (row // block_rows * CORES + which_core) * block_rows + row % block_rows
        match = (value[:, None] == label_row[None, :]).astype(jnp.bfloat16)
        return jnp.dot(match, features, preferred_element_type=jnp.float32)

    away = local_sums(1 - core).astype(jnp.bfloat16)
    sibling = lax.ppermute(away, "region", [(r, r ^ 1) for r in range(region_count)])

    blocks = [memory] + [
        lax.ppermute(memory, "group", [(g, g ^ k) for g in range(group_count)])
        for k in range(1, group_count)
    ]

    all_labels = labels
    step = 1
    while step < region_count:
        all_labels = jnp.concatenate(
            [
                all_labels,
                lax.ppermute(all_labels, "region", [(r, r ^ step) for r in range(region_count)]),
            ]
        )
        step *= 2

    chip_sums = (local_sums(core) + sibling.astype(jnp.float32)).astype(jnp.bfloat16)
    chip_sums = chip_sums.reshape(layers, block_rows, feat_width)

    halves = 2
    half_rows = block_rows // halves
    right = [None] * halves
    left = [None] * halves
    for hop in range(layers - 1):
        up = [
            (z * CORES + c, (z + 1) * CORES + c) for z in range(hop + 1) for c in range(CORES)
        ]
        down = [
            ((layers - 1 - z) * CORES + c, (layers - 2 - z) * CORES + c)
            for z in range(hop + 1)
            for c in range(CORES)
        ]
        up_target = jnp.clip(layers - 1 - hop + layer, 0, layers - 1)
        down_target = jnp.clip(hop - (layers - 1 - layer), 0, layers - 1)
        for h in range(halves):
            def own(target):
                return lax.dynamic_slice(
                    chip_sums, (target, h * half_rows, 0), (1, half_rows, feat_width)
                )[0]

            def joined(target, came):
                if came is None:
                    return own(target)
                return (own(target).astype(jnp.float32) + came.astype(jnp.float32)).astype(
                    jnp.bfloat16
                )

            right[h] = lax.ppermute(joined(up_target, right[h]), "region", up)
            left[h] = lax.ppermute(joined(down_target, left[h]), "region", down)

    wanted_owner = jnp.take(owners[0], requests[0], axis=0) ^ group
    chosen = []
    for k in range(wanted_owner.shape[0]):
        block = blocks[0]
        for j in range(1, group_count):
            block = jnp.where(wanted_owner[k] == j, blocks[j], block)
        chosen.append(block)
    candidates = jnp.concatenate(chosen)
    cand_count = candidates.shape[0]
    scores = (
        lax.dot_general(
            features, candidates, (((1,), (1,)), ((), ())), preferred_element_type=jnp.float32
        )
        / exponent_sharpness
    )
    shifted = scores - jnp.max(scores, axis=1, keepdims=True)
    expo = jnp.exp(shifted)
    likelihoods = expo / jnp.sum(expo, axis=1, keepdims=True)
    column = jnp.arange(cand_count, dtype=jnp.int32)
    target = (
        jnp.where(column < block_rows, (1.0 - smoothing) / block_rows, 0.0) + smoothing / cand_count
    ).astype(jnp.float32)
    logit_grad = ((likelihoods - target[None, :]) / exponent_sharpness).astype(jnp.bfloat16)
    feat_grad = jnp.dot(logit_grad, candidates, preferred_element_type=jnp.float32).astype(
        jnp.bfloat16
    )

    my_rows = region * block_rows + jnp.arange(block_rows, dtype=jnp.int32)
    counts = jnp.sum(
        (my_rows[:, None] == all_labels.reshape(-1)[None, :]).astype(jnp.float32), axis=1
    )
    own_sums = lax.dynamic_index_in_dim(chip_sums, layer, 0, keepdims=False).astype(jnp.float32)
    sums = (
        own_sums
        + jnp.concatenate(right).astype(jnp.float32)
        + jnp.concatenate(left).astype(jnp.float32)
    )
    old_rows = memory.astype(jnp.float32)
    averaged = sums / jnp.maximum(counts, 1.0)[:, None]
    mixed = jnp.where(
        counts[:, None] > 0, momentum_keep * old_rows + (1.0 - momentum_keep) * averaged, old_rows
    )
    scale = lax.rsqrt(jnp.mean(mixed * mixed, axis=1, keepdims=True) + 1e-06) * D ** (-0.5)
    new_memory = (mixed * scale).astype(jnp.bfloat16)
    return (feat_grad, new_memory)


def solution(mesh):
    placed = (
        P(("region", "group"), None),
        P(("region", "group"), None),
        P(("region", "group"), None),
        P("region", None),
        P(("region", "group"), None),
    )
    return jax.shard_map(
        on_device,
        mesh=mesh,
        in_specs=placed,
        out_specs=(P(("region", "group"), None), P(("region", "group"), None)),
        check_vma=False,
    )
```

time: 110 us -> 76.4 us (0.69)
  waiting for transfers between devices: 66.2 us -> 17.3 us
  starting transfers between devices: 10.9 us -> 39 us
  between operations: 14.2 us -> 4.83 us
  local copies, waits for them, and re-layouts: 4.41 us -> 1.92 us
    ppermute x0 -> x19, starting transfers between devices: none -> 39 us  [the longest x6 23.5 us: on_device(): right[h] = lax.ppermute(joined(up_target, right[h]), 'region', up)]
    all_gather x1 -> x0, waiting for transfers between devices: 36.5 us -> none  [on_device(): lax.all_gather(memory, 'group', axis=0, tiled=True)]
    all_to_all x2 -> x0, waiting for transfers between devices: 29 us -> none  [the longest x1 27 us: on_device(): lax.all_to_all(packed, 'region', split_axis=0, concat_axis=0, tiled=True)]
    ppermute x0 -> x19, waiting for transfers between devices: none -> 17.3 us  [the longest x6 9.06 us: on_device(): right[h] = lax.ppermute(joined(up_target, right[h]), 'region', up)]
    all_to_all x2 -> x0, starting transfers between devices: 10.9 us -> none  [the longest x1 6.33 us: on_device(): lax.all_to_all(slot_offsets, 'region', split_axis=0, concat_axis=0, tiled...]
    gather x2 -> x1, local copies, waits for them, and re-layouts: 2.84 us -> 0.64 us  [on_device(): wanted_owner = jnp.take(owners[0], requests[0], axis=0) ^ group]
  transfers between devices with their start and end apart: 3 -> 19, of which waited for: 3 -> 6; matrix products, arithmetic and copies ran while one was open for 10% -> 12% of each run, Pallas kernels for 0% -> 0%
where the time goes in v1:
time: 76.4 us; the launch traced here: 75.9 us
  starting transfers between devices  39 us (51%)
  waiting for transfers between devices  17.3 us (23%)
  matrix products  8.11 us (11%)
  between operations  4.83 us (6%)
  other arithmetic  4.75 us (6%)
  local copies, waits for them, and re-layouts  1.92 us (3%)
    ppermute x6, starting transfers between devices, on_device(): right[h] = lax.ppermute(joined(up_target, right[h]), 'region', up)  23.5 us
    ppermute x6, waiting for transfers between devices, on_device(): right[h] = lax.ppermute(joined(up_target, right[h]), 'region', up)  9.06 us
    ppermute x6, waiting for transfers between devices, on_device(): left[h] = lax.ppermute(joined(down_target, left[h]), 'region', down)  6.63 us
    dot_general x2, matrix products, local_sums(): return jnp.dot(match, features, preferred_element_type=jnp.float32)  5.52 us
    ppermute x6, starting transfers between devices, on_device(): left[h] = lax.ppermute(joined(down_target, left[h]), 'region', down)  5.28 us
    ppermute x3, starting transfers between devices, on_device(): lax.ppermute(all_labels, 'region', [(r, r ^ step) for r in range(region_c...  5.27 us
    ppermute x3, starting transfers between devices, on_device(): lax.ppermute(memory, 'group', [(g, g ^ k) for g in range(group_count)])  4.46 us
    dot_general x1, matrix products, on_device(): jnp.dot(logit_grad, candidates, preferred_element_type=jnp.float32)  1.85 us
  transfers between devices with their start and end apart: 19, of which 6 were waited for; matrix products, arithmetic and copies ran while one was open for 12% of the time, Pallas kernels for 0%

profile of v1, /device:TPU:0, one launch (start us, length us, event | category | flops | bytes accessed | tf_op | source)
XLA Modules:
  0.0 75.9 jit_solution(10915059987273087152)
XLA Ops:
  0.6 0.0 copy-start
  0.7 0.8 %reduce.2 = s32[384]{0:T(512)S(1)} reduce(s32[1,384]{1,0:T(1,128)} %param.9, s32[]{:T(128)} %constant.109.clone.1), dimensions={0}, to_apply=%param.9.reduce_sub_computation | reduce | bytes 3076 | tf_op args[4]
  1.5 0.6 copy-done
  2.1 2.6 %convolution_convert_fusion = bf16[512,2048]{1,0:T(8,128)(2,1)} fusion(bf16[384,2048]{1,0:T(8,128)(2,1)S(1)} %copy-done, s32[384]{0:T(512)S(1)} %reduce.2, s32[512]{0:T(512)S(1)} %multiply_add_fusion), kind=kOutput, calls=%fused_computation.2 | convolution fusion | flops 806551552 | bytes 3673600 | tf_op jit(solution)/shard_map/dot_general | solution.py:28
  4.7 0.5 collective-permute-start.6
  5.2 0.1 collective-permute-start.3
  5.2 3.9 %collective-permute-start = (bf16[128,2048]{1,0:T(8,128)(2,1)S(1)}, bf16[128,2048]{1,0:T(8,128)(2,1)S(1)}, u32[]{:S(2)}, u32[]{:S(2)}) collective-permute-start(bf16[128,2048]{1,0:T(8,128)(2,1)S(1)} %copy-done.2), channel_id=1, source_target_pairs={{0,3},{1,2},{2,1},{3,0},{4,7},{5,6},{6,5},{7,4},{8,11},{9,10},{10,... | collective-permute-start | bytes 1572872 | tf_op jit(solution)/shard_map/ppermute | solution.py:34
  9.1 0.5 collective-permute-start.1
  9.6 0.1 collective-permute-start.2
  9.7 0.6 gather_fusion
  10.4 0.6 fusion.40
  10.9 0.0 collective-permute-done.3
  11.0 2.1 %collective-permute-start.4 = (s32[2,384]{1,0:T(2,128)S(1)}, s32[2,384]{1,0:T(2,128)S(1)}, u32[]{:S(2)}, u32[]{:S(2)}) collective-permute-start(s32[2,384]{1,0:T(2,128)S(1)} %pad_add_fusion.2), channel_id=1, source_target_pairs={{0,8},{4,12},{8,0},{12,4},{16,24},{20,28},{24,16},{28,20},{1,9},{5... | collective-permute-start | bytes 9224 | tf_op jit(solution)/shard_map/ppermute | solution.py:44
  13.1 1.6 %collective-permute-done.4 = s32[2,384]{1,0:T(2,128)S(1)} collective-permute-done((s32[2,384]{1,0:T(2,128)S(1)}, s32[2,384]{1,0:T(2,128)S(1)}, u32[]{:S(2)}, u32[]{:S(2)}) %collective-permute-start.4) | collective-permute-done | bytes 3104 | tf_op jit(solution)/shard_map/ppermute | solution.py:44
  14.7 3.1 %collective-permute-start.5 = (s32[4,384]{1,0:T(4,128)S(1)}, s32[4,384]{1,0:T(4,128)S(1)}, u32[]{:S(2)}, u32[]{:S(2)}) collective-permute-start(s32[4,384]{1,0:T(4,128)S(1)} %pad_add_fusion.1), channel_id=1, source_target_pairs={{0,16},{4,20},{8,24},{12,28},{16,0},{20,4},{24,8},{28,12},{1,17},{... | collective-permute-start | bytes 18440 | tf_op jit(solution)/shard_map/ppermute | solution.py:44
  21.7 0.3 convert_reduce_fusion
  22.0 2.9 %add_convert_fusion = bf16[512,2048]{1,0:T(8,128)(2,1)S(1)} fusion(bf16[512,2048]{1,0:T(8,128)(2,1)} %collective-permute-done.6, bf16[384,2048]{1,0:T(8,128)(2,1)S(1)} %copy-done, s32[384]{0:T(512)S(1)} %reduce.2, s32[512]{0:T(512)S(1)} %multiply_add_fusion.1), kind=kOutput, calls=%fused_computation.1 | convolution fusion | flops 808648704 | bytes 5770752 | tf_op jit(solution)/shard_map/dot_general | solution.py:28
  24.9 0.1 dynamic-slice_bitcast_fusion.3
  25.0 3.5 %collective-permute-start.7 = (bf16[64,2048]{1,0:T(8,128)(2,1)S(1)}, bf16[64,2048]{1,0:T(8,128)(2,1)S(1)}, u32[]{:S(2)}, u32[]{:S(2)}) collective-permute-start(bf16[64,2048]{1,0:T(8,128)(2,1)S(1)} %get-tuple-element.8), channel_id=1, source_target_pairs={{0,8},{4,12},{1,9},{5,13},{2,10},{6,14},{3,11},{7,15}} | collective-permute-start | bytes 786440 | tf_op jit(solution)/shard_map/ppermute | solution.py:80
  28.6 1.3 %collective-permute-start.10 = (bf16[64,2048]{1,0:T(8,128)(2,1)S(1)}, bf16[64,2048]{1,0:T(8,128)(2,1)S(1)}, u32[]{:S(2)}, u32[]{:S(2)}) collective-permute-start(bf16[64,2048]{1,0:T(8,128)(2,1)S(1)} %get-tuple-element.11), channel_id=1, source_target_pairs={{0,8},{4,12},{1,9},{5,13},{2,10},{6,14},{3,11},{7,15}} | collective-permute-start | bytes 786440 | tf_op jit(solution)/shard_map/ppermute | solution.py:80
  29.9 5.3 %collective-permute-done.7 = bf16[64,2048]{1,0:T(8,128)(2,1)S(1)} collective-permute-done((bf16[64,2048]{1,0:T(8,128)(2,1)S(1)}, bf16[64,2048]{1,0:T(8,128)(2,1)S(1)}, u32[]{:S(2)}, u32[]{:S(2)}) %collective-permute-start.7) | collective-permute-done | bytes 262176 | tf_op jit(solution)/shard_map/ppermute | solution.py:80
  35.1 0.7 collective-permute-start.13
  35.8 0.1 fusion.15
  35.9 0.0 collective-permute-done
  35.9 0.7 collective-permute-start.16
  36.6 4.4 %collective-permute-start.8 = (bf16[64,2048]{1,0:T(8,128)(2,1)S(1)}, bf16[64,2048]{1,0:T(8,128)(2,1)S(1)}, u32[]{:S(2)}, u32[]{:S(2)}) collective-permute-start(bf16[64,2048]{1,0:T(8,128)(2,1)S(1)} %fusion.15), channel_id=1, source_target_pairs={{0,8},{4,12},{8,16},{12,20},{1,9},{5,13},{9,17},{13,21},{2,10},{6,... | collective-permute-start | bytes 786440 | tf_op jit(solution)/shard_map/ppermute | solution.py:80
  41.0 1.2 %select_select_fusion.1 = (bf16[128,2048]{1,0:T(8,128)(2,1)S(1)}, bf16[128,2048]{1,0:T(8,128)(2,1)S(1)}) fusion(bf16[128,2048]{1,0:T(8,128)(2,1)S(1)} %collective-permute-done, bf16[128,2048]{1,0:T(8,128)(2,1)S(1)} %collective-permute-done.1, bf16[128,2048]{1,0:T(8,128)(2,1)} %collective-permute-done.2, bf16[128,2048]{1,0:T(8,128)(2,1)S(1)} %copy-done.2, ...), kind=kLoop, calls=%fused_computation.36 | loop fusion | flops 1572864 | bytes 3145734 | tf_op jit(solution)/shard_map/jit(_where)/select_n | solution.py:88
  42.3 0.0 collective-permute-done.13
  42.3 0.0 collective-permute-done.16
  42.3 2.6 %collective-permute-done.8 = bf16[64,2048]{1,0:T(8,128)(2,1)S(1)} collective-permute-done((bf16[64,2048]{1,0:T(8,128)(2,1)S(1)}, bf16[64,2048]{1,0:T(8,128)(2,1)S(1)}, u32[]{:S(2)}, u32[]{:S(2)}) %collective-permute-start.8) | collective-permute-done | bytes 262176 | tf_op jit(solution)/shard_map/ppermute | solution.py:80
  44.9 0.4 fusion.16
  45.3 4.4 %collective-permute-start.11 = (bf16[64,2048]{1,0:T(8,128)(2,1)S(1)}, bf16[64,2048]{1,0:T(8,128)(2,1)S(1)}, u32[]{:S(2)}, u32[]{:S(2)}) collective-permute-start(bf16[64,2048]{1,0:T(8,128)(2,1)S(1)} %get-tuple-element.7), channel_id=1, source_target_pairs={{0,8},{4,12},{8,16},{12,20},{1,9},{5,13},{9,17},{13,21},{2,10},{6,... | collective-permute-start | bytes 786440 | tf_op jit(solution)/shard_map/ppermute | solution.py:80
  49.7 0.7 collective-permute-start.14
  50.4 0.7 collective-permute-start.17
  51.0 0.7 fusion.41
  51.8 0.1 fusion.21
  51.9 3.1 %collective-permute-start.9 = (bf16[64,2048]{1,0:T(8,128)(2,1)S(1)}, bf16[64,2048]{1,0:T(8,128)(2,1)S(1)}, u32[]{:S(2)}, u32[]{:S(2)}) collective-permute-start(bf16[64,2048]{1,0:T(8,128)(2,1)S(1)} %get-tuple-element.4), channel_id=1, source_target_pairs={{0,8},{4,12},{8,16},{12,20},{16,24},{20,28},{1,9},{5,13},{9,17},{1... | collective-permute-start | bytes 786440 | tf_op jit(solution)/shard_map/ppermute | solution.py:80
  55.0 1.2 %collective-permute-done.11 = bf16[64,2048]{1,0:T(8,128)(2,1)S(1)} collective-permute-done((bf16[64,2048]{1,0:T(8,128)(2,1)S(1)}, bf16[64,2048]{1,0:T(8,128)(2,1)S(1)}, u32[]{:S(2)}, u32[]{:S(2)}) %collective-permute-start.11) | collective-permute-done | bytes 262176 | tf_op jit(solution)/shard_map/ppermute | solution.py:80
  56.2 0.0 collective-permute-done.14
  56.2 0.3 fusion.14
  56.5 6.8 %collective-permute-start.12 = (bf16[64,2048]{1,0:T(8,128)(2,1)S(1)}, bf16[64,2048]{1,0:T(8,128)(2,1)S(1)}, u32[]{:S(2)}, u32[]{:S(2)}) collective-permute-start(bf16[64,2048]{1,0:T(8,128)(2,1)S(1)} %get-tuple-element.12), channel_id=1, source_target_pairs={{0,8},{4,12},{8,16},{12,20},{16,24},{20,28},{1,9},{5,13},{9,17},{1... | collective-permute-start | bytes 786440 | tf_op jit(solution)/shard_map/ppermute | solution.py:80
  63.3 1.3 %collective-permute-start.15 = (bf16[64,2048]{1,0:T(8,128)(2,1)S(1)}, bf16[64,2048]{1,0:T(8,128)(2,1)S(1)}, u32[]{:S(2)}, u32[]{:S(2)}) collective-permute-start(bf16[64,2048]{1,0:T(8,128)(2,1)S(1)} %get-tuple-element.14), channel_id=1, source_target_pairs={{24,16},{28,20},{16,8},{20,12},{8,0},{12,4},{25,17},{29,21},{17,9}... | collective-permute-start | bytes 786440 | tf_op jit(solution)/shard_map/ppermute | solution.py:81
  64.6 1.3 %collective-permute-start.18 = (bf16[64,2048]{1,0:T(8,128)(2,1)S(1)}, bf16[64,2048]{1,0:T(8,128)(2,1)S(1)}, u32[]{:S(2)}, u32[]{:S(2)}) collective-permute-start(bf16[64,2048]{1,0:T(8,128)(2,1)S(1)} %get-tuple-element.13), channel_id=1, source_target_pairs={{24,16},{28,20},{16,8},{20,12},{8,0},{12,4},{25,17},{29,21},{17,9}... | collective-permute-start | bytes 786440 | tf_op jit(solution)/shard_map/ppermute | solution.py:81
  65.9 1.8 %convolution_convert_fusion.1 = bf16[384,2048]{1,0:T(8,128)(2,1)} fusion(bf16[128,2048]{1,0:T(8,128)(2,1)S(1)} %get-tuple-element.16, bf16[128,2048]{1,0:T(8,128)(2,1)S(1)} %get-tuple-element.15, f32[256,384]{1,0:T(8,128)S(1)} %get-tuple-element.20, f32[256]{0:T(256)S(1)} %fusion.34, f32[384]{0:T(512)S(1)} %fusion.21, f32[384]{0:T(512)S(1)} %get-tuple-element.19), kind=kOutput, calls=%fused_computation.3 | convolution fusion | flops 406028288 | bytes 3018752 | tf_op jit(solution)/shard_map/dot_general | solution.py:106
  67.8 3.8 %collective-permute-done.15 = bf16[64,2048]{1,0:T(8,128)(2,1)S(1)} collective-permute-done((bf16[64,2048]{1,0:T(8,128)(2,1)S(1)}, bf16[64,2048]{1,0:T(8,128)(2,1)S(1)}, u32[]{:S(2)}, u32[]{:S(2)}) %collective-permute-start.15) | collective-permute-done | bytes 262176 | tf_op jit(solution)/shard_map/ppermute | solution.py:81
  71.6 2.8 %collective-permute-done.18 = bf16[64,2048]{1,0:T(8,128)(2,1)S(1)} collective-permute-done((bf16[64,2048]{1,0:T(8,128)(2,1)S(1)}, bf16[64,2048]{1,0:T(8,128)(2,1)S(1)}, u32[]{:S(2)}, u32[]{:S(2)}) %collective-permute-start.18) | collective-permute-done | bytes 262176 | tf_op jit(solution)/shard_map/ppermute | solution.py:81
  74.4 0.6 multiply_reduce_fusion
  75.0 0.9 %multiply_convert_fusion = bf16[128,2048]{1,0:T(8,128)(2,1)} fusion(f32[128,2048]{1,0:T(8,128)S(1)} %get-tuple-element.3, f32[128]{0:T(128)S(1)} %rsqrt_multiply_fusion), kind=kLoop, calls=%fused_computation.14 | loop fusion | flops 524288 | bytes 1573376 | tf_op jit(solution)/shard_map/convert_element_type | solution.py:126
  (30 shorter events, 0.1 us)
Async XLA Ops:
  0.6 1.4 %copy-start = (bf16[384,2048]{1,0:T(8,128)(2,1)S(1)}, bf16[384,2048]{1,0:T(8,128)(2,1)}, u32[]{:S(2)}) copy-start(bf16[384,2048]{1,0:T(8,128)(2,1)} %param.5) | copy-start | bytes 4718596
  2.1 3.1 %copy-start.3 = (s32[1,384]{1,0:T(1,128)S(1)}, s32[1,384]{1,0:T(1,128)}, u32[]{:S(2)}) copy-start(s32[1,384]{1,0:T(1,128)} %param.9) | copy-start | bytes 4612
  2.1 3.2 %copy-start.2 = (bf16[128,2048]{1,0:T(8,128)(2,1)S(1)}, bf16[128,2048]{1,0:T(8,128)(2,1)}, u32[]{:S(2)}) copy-start(bf16[128,2048]{1,0:T(8,128)(2,1)} %param.6) | copy-start | bytes 1572868
  2.1 7.6 %copy-start.4 = (s32[1,2]{1,0:T(1,128)S(1)}, s32[1,2]{1,0:T(1,128)}, u32[]{:S(2)}) copy-start(s32[1,2]{1,0:T(1,128)} %param.7) | copy-start | bytes 28
  2.1 7.6 %copy-start.1 = (s32[1,4]{1,0:T(1,128)S(1)}, s32[1,4]{1,0:T(1,128)}, u32[]{:S(2)}) copy-start(s32[1,4]{1,0:T(1,128)} %param.8) | copy-start | bytes 52
  4.7 17.3 %collective-permute-start.6 = (bf16[512,2048]{1,0:T(8,128)(2,1)}, bf16[512,2048]{1,0:T(8,128)(2,1)}, u32[]{:S(2)}, u32[]{:S(2)}) collective-permute-start(bf16[512,2048]{1,0:T(8,128)(2,1)} %convolution_convert_fusion), channel_id=1, source_target_pairs={{0,4},{4,0},{8,12},{12,8},{16,20},{20,16},{24,28},{28,24},{1,5},{5... | collective-permute-start | bytes 6291464 | tf_op jit(solution)/shard_map/ppermute | solution.py:31
  5.2 5.8 %collective-permute-start.3 = (s32[1,384]{1,0:T(1,128)S(1)}, s32[1,384]{1,0:T(1,128)S(1)}, u32[]{:S(2)}, u32[]{:S(2)}) collective-permute-start(s32[1,384]{1,0:T(1,128)S(1)} %copy-done.3), channel_id=1, source_target_pairs={{0,4},{4,0},{8,12},{12,8},{16,20},{20,16},{24,28},{28,24},{1,5},{5... | collective-permute-start | bytes 4616 | tf_op jit(solution)/shard_map/ppermute | solution.py:44
  5.2 30.7 %collective-permute-start = (bf16[128,2048]{1,0:T(8,128)(2,1)S(1)}, bf16[128,2048]{1,0:T(8,128)(2,1)S(1)}, u32[]{:S(2)}, u32[]{:S(2)}) collective-permute-start(bf16[128,2048]{1,0:T(8,128)(2,1)S(1)} %copy-done.2), channel_id=1, source_target_pairs={{0,3},{1,2},{2,1},{3,0},{4,7},{5,6},{6,5},{7,4},{8,11},{9,10},{10,... | collective-permute-start | bytes 1572872 | tf_op jit(solution)/shard_map/ppermute | solution.py:34
  9.1 27.5 %collective-permute-start.1 = (bf16[128,2048]{1,0:T(8,128)(2,1)S(1)}, bf16[128,2048]{1,0:T(8,128)(2,1)S(1)}, u32[]{:S(2)}, u32[]{:S(2)}) collective-permute-start(bf16[128,2048]{1,0:T(8,128)(2,1)S(1)} %copy-done.2), channel_id=1, source_target_pairs={{0,2},{1,3},{2,0},{3,1},{4,6},{5,7},{6,4},{7,5},{8,10},{9,11},{10,... | collective-permute-start | bytes 1572872 | tf_op jit(solution)/shard_map/ppermute | solution.py:34
  9.6 31.4 %collective-permute-start.2 = (bf16[128,2048]{1,0:T(8,128)(2,1)S(1)}, bf16[128,2048]{1,0:T(8,128)(2,1)}, u32[]{:S(2)}, u32[]{:S(2)}) collective-permute-start(bf16[128,2048]{1,0:T(8,128)(2,1)S(1)} %copy-done.2), channel_id=1, source_target_pairs={{0,1},{1,0},{2,3},{3,2},{4,5},{5,4},{6,7},{7,6},{8,9},{9,8},{10,11... | collective-permute-start | bytes 1572872 | tf_op jit(solution)/shard_map/ppermute | solution.py:34
  11.0 3.7 %collective-permute-start.4 = (s32[2,384]{1,0:T(2,128)S(1)}, s32[2,384]{1,0:T(2,128)S(1)}, u32[]{:S(2)}, u32[]{:S(2)}) collective-permute-start(s32[2,384]{1,0:T(2,128)S(1)} %pad_add_fusion.2), channel_id=1, source_target_pairs={{0,8},{4,12},{8,0},{12,4},{16,24},{20,28},{24,16},{28,20},{1,9},{5... | collective-permute-start | bytes 9224 | tf_op jit(solution)/shard_map/ppermute | solution.py:44
  14.7 7.0 %collective-permute-start.5 = (s32[4,384]{1,0:T(4,128)S(1)}, s32[4,384]{1,0:T(4,128)S(1)}, u32[]{:S(2)}, u32[]{:S(2)}) collective-permute-start(s32[4,384]{1,0:T(4,128)S(1)} %pad_add_fusion.1), channel_id=1, source_target_pairs={{0,16},{4,20},{8,24},{12,28},{16,0},{20,4},{24,8},{28,12},{1,17},{... | collective-permute-start | bytes 18440 | tf_op jit(solution)/shard_map/ppermute | solution.py:44
  25.0 10.1 %collective-permute-start.7 = (bf16[64,2048]{1,0:T(8,128)(2,1)S(1)}, bf16[64,2048]{1,0:T(8,128)(2,1)S(1)}, u32[]{:S(2)}, u32[]{:S(2)}) collective-permute-start(bf16[64,2048]{1,0:T(8,128)(2,1)S(1)} %get-tuple-element.8), channel_id=1, source_target_pairs={{0,8},{4,12},{1,9},{5,13},{2,10},{6,14},{3,11},{7,15}} | collective-permute-start | bytes 786440 | tf_op jit(solution)/shard_map/ppermute | solution.py:80
  28.6 13.7 %collective-permute-start.10 = (bf16[64,2048]{1,0:T(8,128)(2,1)S(1)}, bf16[64,2048]{1,0:T(8,128)(2,1)S(1)}, u32[]{:S(2)}, u32[]{:S(2)}) collective-permute-start(bf16[64,2048]{1,0:T(8,128)(2,1)S(1)} %get-tuple-element.11), channel_id=1, source_target_pairs={{0,8},{4,12},{1,9},{5,13},{2,10},{6,14},{3,11},{7,15}} | collective-permute-start | bytes 786440 | tf_op jit(solution)/shard_map/ppermute | solution.py:80
  35.1 7.1 %collective-permute-start.13 = (bf16[64,2048]{1,0:T(8,128)(2,1)S(1)}, bf16[64,2048]{1,0:T(8,128)(2,1)S(1)}, u32[]{:S(2)}, u32[]{:S(2)}) collective-permute-start(bf16[64,2048]{1,0:T(8,128)(2,1)S(1)} %get-tuple-element.10), channel_id=1, source_target_pairs={{24,16},{28,20},{25,17},{29,21},{26,18},{30,22},{27,19},{31,23}} | collective-permute-start | bytes 786440 | tf_op jit(solution)/shard_map/ppermute | solution.py:81
  35.9 6.4 %collective-permute-start.16 = (bf16[64,2048]{1,0:T(8,128)(2,1)S(1)}, bf16[64,2048]{1,0:T(8,128)(2,1)S(1)}, u32[]{:S(2)}, u32[]{:S(2)}) collective-permute-start(bf16[64,2048]{1,0:T(8,128)(2,1)S(1)} %get-tuple-element.9), channel_id=1, source_target_pairs={{24,16},{28,20},{25,17},{29,21},{26,18},{30,22},{27,19},{31,23}} | collective-permute-start | bytes 786440 | tf_op jit(solution)/shard_map/ppermute | solution.py:81
  36.6 8.3 %collective-permute-start.8 = (bf16[64,2048]{1,0:T(8,128)(2,1)S(1)}, bf16[64,2048]{1,0:T(8,128)(2,1)S(1)}, u32[]{:S(2)}, u32[]{:S(2)}) collective-permute-start(bf16[64,2048]{1,0:T(8,128)(2,1)S(1)} %fusion.15), channel_id=1, source_target_pairs={{0,8},{4,12},{8,16},{12,20},{1,9},{5,13},{9,17},{13,21},{2,10},{6,... | collective-permute-start | bytes 786440 | tf_op jit(solution)/shard_map/ppermute | solution.py:80
  45.3 11.0 %collective-permute-start.11 = (bf16[64,2048]{1,0:T(8,128)(2,1)S(1)}, bf16[64,2048]{1,0:T(8,128)(2,1)S(1)}, u32[]{:S(2)}, u32[]{:S(2)}) collective-permute-start(bf16[64,2048]{1,0:T(8,128)(2,1)S(1)} %get-tuple-element.7), channel_id=1, source_target_pairs={{0,8},{4,12},{8,16},{12,20},{1,9},{5,13},{9,17},{13,21},{2,10},{6,... | collective-permute-start | bytes 786440 | tf_op jit(solution)/shard_map/ppermute | solution.py:80
  49.7 6.6 %collective-permute-start.14 = (bf16[64,2048]{1,0:T(8,128)(2,1)S(1)}, bf16[64,2048]{1,0:T(8,128)(2,1)S(1)}, u32[]{:S(2)}, u32[]{:S(2)}) collective-permute-start(bf16[64,2048]{1,0:T(8,128)(2,1)S(1)} %get-tuple-element.6), channel_id=1, source_target_pairs={{24,16},{28,20},{16,8},{20,12},{25,17},{29,21},{17,9},{21,13},{26,... | collective-permute-start | bytes 786440 | tf_op jit(solution)/shard_map/ppermute | solution.py:81
  50.4 5.9 %collective-permute-start.17 = (bf16[64,2048]{1,0:T(8,128)(2,1)S(1)}, bf16[64,2048]{1,0:T(8,128)(2,1)S(1)}, u32[]{:S(2)}, u32[]{:S(2)}) collective-permute-start(bf16[64,2048]{1,0:T(8,128)(2,1)S(1)} %get-tuple-element.5), channel_id=1, source_target_pairs={{24,16},{28,20},{16,8},{20,12},{25,17},{29,21},{17,9},{21,13},{26,... | collective-permute-start | bytes 786440 | tf_op jit(solution)/shard_map/ppermute | solution.py:81
  51.9 15.9 %collective-permute-start.9 = (bf16[64,2048]{1,0:T(8,128)(2,1)S(1)}, bf16[64,2048]{1,0:T(8,128)(2,1)S(1)}, u32[]{:S(2)}, u32[]{:S(2)}) collective-permute-start(bf16[64,2048]{1,0:T(8,128)(2,1)S(1)} %get-tuple-element.4), channel_id=1, source_target_pairs={{0,8},{4,12},{8,16},{12,20},{16,24},{20,28},{1,9},{5,13},{9,17},{1... | collective-permute-start | bytes 786440 | tf_op jit(solution)/shard_map/ppermute | solution.py:80
  56.5 11.3 %collective-permute-start.12 = (bf16[64,2048]{1,0:T(8,128)(2,1)S(1)}, bf16[64,2048]{1,0:T(8,128)(2,1)S(1)}, u32[]{:S(2)}, u32[]{:S(2)}) collective-permute-start(bf16[64,2048]{1,0:T(8,128)(2,1)S(1)} %get-tuple-element.12), channel_id=1, source_target_pairs={{0,8},{4,12},{8,16},{12,20},{16,24},{20,28},{1,9},{5,13},{9,17},{1... | collective-permute-start | bytes 786440 | tf_op jit(solution)/shard_map/ppermute | solution.py:80
  63.3 8.3 %collective-permute-start.15 = (bf16[64,2048]{1,0:T(8,128)(2,1)S(1)}, bf16[64,2048]{1,0:T(8,128)(2,1)S(1)}, u32[]{:S(2)}, u32[]{:S(2)}) collective-permute-start(bf16[64,2048]{1,0:T(8,128)(2,1)S(1)} %get-tuple-element.14), channel_id=1, source_target_pairs={{24,16},{28,20},{16,8},{20,12},{8,0},{12,4},{25,17},{29,21},{17,9}... | collective-permute-start | bytes 786440 | tf_op jit(solution)/shard_map/ppermute | solution.py:81
  64.6 9.8 %collective-permute-start.18 = (bf16[64,2048]{1,0:T(8,128)(2,1)S(1)}, bf16[64,2048]{1,0:T(8,128)(2,1)S(1)}, u32[]{:S(2)}, u32[]{:S(2)}) collective-permute-start(bf16[64,2048]{1,0:T(8,128)(2,1)S(1)} %get-tuple-element.13), channel_id=1, source_target_pairs={{24,16},{28,20},{16,8},{20,12},{8,0},{12,4},{25,17},{29,21},{17,9}... | collective-permute-start | bytes 786440 | tf_op jit(solution)/shard_map/ppermute | solution.py:81
